TPU v7x, 256 devices: a whole 4x4x8 slice. The times are simulated.
256 devices in a mesh: mesh: 32 (over x, z), harm: 8 (over y, core).
Axes of the slice: x: 4, y: 4, z: 8, core: 2. Of those that a mesh axis runs over, the one named last changes fastest.
Arguments:
- adjoint_rhs: float32 [16, 6, 2, 65536], P('harm', None, None, 'mesh'), may hold values from -20 to 20
- forward_field: float32 [16, 2, 65536], P('harm', None, 'mesh'), may hold values from -6 to 6
- stiffness: float32 [64, 64, 4096], P(None, None, 'mesh'), may hold values from -1 to 3, as said below
- mass_blocks: float32 [64, 64, 4096], P(None, None, 'mesh'), may hold values from -1 to 3, as said below
- frequency: float32 [16], P('harm'), may hold values from 0.25 to 4
- edge_mass: float32 [65536], P('mesh'), may hold values from 0.5 to 2
- connectivity: int32 [64, 4096], P(None, 'mesh'), may hold values from 0 to 3071, as said below
- send_list: int32 [32, 2, 512], P('mesh'), may hold values from -1 to 2047, as said below
- node_block: int32 [32768], P('mesh'), may hold values from 0 to 127
- node_shape: float32 [3, 64, 32768], P(None, None, 'mesh'), may hold values from -0.1875 to 0.1875
Outputs:
- adjoint: float32 [16, 6, 2, 65536], P('harm', None, None, 'mesh')
- shape_gradient: float32 [6, 3, 32768], P(None, None, ('mesh', 'harm'))
Inputs may be any that keep to these rules, and one draw needn't show every extreme that they name: `stiffness`: each block is symmetric and its diagonal exceeds the sum of magnitudes of the other entries of its row. `mass_blocks`: each block is symmetric and its diagonal exceeds the sum of magnitudes of the other entries of its row. `send_list`: row 0 of a device lists owned edges shared with the device one lower along mesh, row 1 those shared with the device one higher; valid entries come first, then -1. A list holds at most 512 valid entries, and some device's row 0 and some device's row 1 hold exactly 512. The first device's row 0 and the last device's row 1 are empty. `connectivity`: an entry below 2048 is an edge the device owns; 2048 + k is entry k of the lower neighbour's row 1; 2560 + k is entry k of the upper neighbour's row 0. Only valid entries are named.
All inputs are finite; a program needn't handle non-finite values.
Results may differ from a plain program's by a relative error of at most 0.0003.
Values sent between devices are 32-bit elements; how exact they have to be, the bound alone decides.
No kernel may reach another device: no remote copies, remote signals or barrier semaphores. Data moves between devices by JAX's collectives and lax.ppermute only.
A program may use at most 128 MiB of HBM per device.

v0:
```python
import jax
import jax.numpy as jnp
from jax import lax
from jax.sharding import PartitionSpec as P

ITERS = 3
exact_mode = lax.Precision.HIGHEST


def extended_2(cells, sides, width):
    for axis, dim in sides:
        count = lax.axis_size(axis)
        ends = count - 1
        head = lax.slice_in_dim(cells, 0, width, axis=dim)
        tail = lax.slice_in_dim(cells, cells.shape[dim] - width, cells.shape[dim], axis=dim)
        cells = jnp.concatenate(
            [
                lax.ppermute(tail, axis, [(i, (i + 1) % count) for i in range(ends)]),
                cells,
                lax.ppermute(head, axis, [((i + 1) % count, i) for i in range(ends)]),
            ],
            axis=dim,
        )
    return cells


def from_behind(shard, axis, by):
    devices = lax.axis_size(axis)
    pairs = [(i, i + by) for i in range(devices) if 0 <= i + by < devices]
    return lax.ppermute(shard, axis, pairs)


def block_product(matrices, gathered):
    return jnp.einsum("ijb,rjb->rib", matrices, gathered, precision=exact_mode)


def per_device(
    adjoint_rhs,
    forward_field,
    stiffness,
    mass_blocks,
    frequency,
    edge_mass,
    connectivity,
    send_list,
    node_block,
    node_shape,
):
    harm_local, force_count, part_count, edge_count = adjoint_rhs.shape
    slot_count = send_list.shape[2]
    row_count = harm_local * force_count * part_count
    list_rows = send_list[0]
    is_listed = list_rows >= 0
    safe_rows = jnp.maximum(list_rows, 0)
    row_weights = jnp.repeat(frequency, force_count * part_count)
    field_weights = jnp.repeat(frequency, part_count)

    def fetch_rim(values_now):
        picked = jnp.where(is_listed[None], values_now[:, safe_rows], 0.0)
        send_buffer = picked.reshape(values_now.shape[0], 2 * slot_count)
        padded = extended_2(send_buffer, (("mesh", 1),), slot_count)
        return jnp.concatenate([padded[:, :slot_count], padded[:, 3 * slot_count :]], axis=1)

    def assemble(values_now, rim_now, weights):
        extended = jnp.concatenate([values_now, rim_now], axis=1)
        gathered = extended[:, connectivity]
        return block_product(stiffness, gathered) + weights[:, None, None] * block_product(
            mass_blocks, gathered
        )

    rhs_rows = adjoint_rhs.reshape(row_count, edge_count)
    field_rows = forward_field.reshape(harm_local * part_count, edge_count)
    first_rim = fetch_rim(rhs_rows)
    solution = jnp.zeros_like(rhs_rows)
    residual = rhs_rows

    def squares(values_now):
        return lax.psum(jnp.sum(values_now * values_now), ("mesh", "harm"))

    direction = residual
    norm_now = squares(residual)
    for iteration in range(ITERS):
        rim_now = first_rim if iteration == 0 else fetch_rim(direction)
        rows_now = direction.shape[0]
        local_terms = assemble(direction, rim_now, row_weights)
        totals = jnp.zeros((rows_now, edge_count + 2 * slot_count), jnp.float32)
        totals = totals.at[:, connectivity.reshape(-1)].add(local_terms.reshape(rows_now, -1))
        owned = totals[:, :edge_count]
        from_upper = from_behind(totals[:, edge_count : edge_count + slot_count], "mesh", -1)
        from_lower = from_behind(totals[:, edge_count + slot_count :], "mesh", 1)
        owned = owned.at[:, safe_rows[1]].add(jnp.where(is_listed[1][None], from_upper, 0.0))
        owned = owned.at[:, safe_rows[0]].add(jnp.where(is_listed[0][None], from_lower, 0.0))
        applied = owned + row_weights[:, None] * edge_mass[None, :] * direction
        step_size = norm_now / lax.psum(jnp.sum(direction * applied), ("mesh", "harm"))
        solution = solution + step_size * direction
        residual = residual - step_size * applied
        norm_next = squares(residual)
        direction = residual + norm_next / norm_now * direction
        norm_now = norm_next
    final_rims = fetch_rim(jnp.concatenate([solution, field_rows], axis=0))
    solution_rim = final_rims[:row_count]
    field_rim = final_rims[row_count:]
    block_edges, block_count = connectivity.shape
    field_terms = assemble(field_rows, field_rim, field_weights).reshape(
        harm_local, part_count, block_edges, block_count
    )
    adjoint_blocks = jnp.concatenate([solution, solution_rim], axis=1)[:, connectivity]
    adjoint_blocks = adjoint_blocks.reshape(
        harm_local, force_count, part_count, block_edges, block_count
    )
    energy_term = jnp.sum(
        adjoint_blocks[:, :, 0] * field_terms[:, None, 0]
        - adjoint_blocks[:, :, 1] * field_terms[:, None, 1],
        axis=0,
    )
    at_nodes = energy_term[:, :, node_block]
    local_grad = -jnp.einsum("kjn,ojn->okn", node_shape, at_nodes, precision=exact_mode)
    summed = lax.psum(local_grad, "harm")
    share_size = local_grad.shape[2] // lax.axis_size("harm")
    gradient = lax.dynamic_slice_in_dim(summed, lax.axis_index("harm") * share_size, share_size, 2)
    return (solution.reshape(adjoint_rhs.shape), gradient)


def solution(mesh):
    return jax.shard_map(
        per_device,
        mesh=mesh,
        in_specs=(
            P("harm", None, None, "mesh"),
            P("harm", None, "mesh"),
            P(None, None, "mesh"),
            P(None, None, "mesh"),
            P("harm"),
            P("mesh"),
            P(None, "mesh"),
            P("mesh", None, None),
            P("mesh"),
            P(None, None, "mesh"),
        ),
        out_specs=(P("harm", None, None, "mesh"), P(None, None, ("mesh", "harm"))),
        check_vma=False,
    )
```

profile of v0, /device:TPU:2, one launch (start us, length us, event | category | flops | bytes accessed | tf_op | source)
XLA Modules:
  0.0 1010.0 jit_solution(11621693017519007216)
XLA Ops:
  10.6 4.0 gather_fusion
  19.6 3.8 collective-permute-start
  23.4 5.8 collective-permute-start.1
  31.7 4.5 copy.190
  36.4 5.6 copy.191
  44.0 27.7 %gather_fusion.1 = f32[8192,24]{1,0:T(8,128)} fusion(f32[24,3072]{0,1:T(8,128)S(1)} %pad_maximum_fusion, s32[8192]{0:T(1024)S(1)} %fusion.70), kind=kCustom, calls=%fused_computation.1 | custom fusion | bytes 1605632 | tf_op jit(solution)/shard_map/gather | solution.py:66
  71.7 3.6 copy.189
  75.4 8.8 fusion.12
  84.1 7.9 add_bitcast_fusion.2
  97.0 44.7 %scatter_custom_fusion = f32[24,3072]{0,1:T(8,128)S(1)} fusion(s32[8192]{0:T(1024)S(1)} %bitcast.176, f32[8192,24]{1,0:T(8,128)} %copy.193, f32[]{:T(128)} %constant.7.clone.1), kind=kCustom, calls=%fused_computation.48 | custom fusion | flops 196608 | bytes 295424 | tf_op jit(solution)/shard_map/scatter-add | solution.py:87
  145.1 3.9 collective-permute-start.2
  151.4 3.6 collective-permute-done.2
  155.0 3.8 scatter_custom_fusion.1
  160.3 15.4 %scatter_custom_fusion.2 = f32[24,2048]{0,1:T(8,128)S(1)} fusion(f32[24,2048]{0,1:T(8,128)S(1)} %scatter_custom_fusion.1, s32[512]{0:T(512)S(1)} %bitcast.180, f32[24,512]{0,1:T(8,128)S(1)} %collective-permute-done.3, f32[]{:T(128)} %constant.7.clone.1, pred[512]{0:T(512)(128)(4,1)S(1)} %get-tuple-element.14), kind=kCustom, calls=%fused_computation.74 | custom fusion | flops 24576 | bytes 459268 | tf_op jit(solution)/shard_map/scatter-add | solution.py:92
  176.9 74.6 %all-reduce = (f32[]{:T(128)}, f32[]{:T(128)}) all-reduce(f32[]{:T(128)} %multiply_reduce_fusion.5, f32[]{:T(128)} %multiply_reduce_fusion), channel_id=1, replica_groups=mesh['mesh'=32,'harm'=8] {'mesh','harm'}, use_global_device_ids=true, to_apply=%region_1.2 | all-reduce | flops 2 | bytes 16 | tf_op jit(solution)/shard_map/psum | solution.py:78
  253.3 73.8 %psum.51 = f32[]{:T(128)} all-reduce(f32[]{:T(128)} %get-tuple-element.18), channel_id=1, replica_groups=mesh['mesh'=32,'harm'=8] {'mesh','harm'}, use_global_device_ids=true, to_apply=%region_8.9 | all-reduce | flops 1 | bytes 8 | tf_op jit(solution)/shard_map/psum | solution.py:78
  331.7 3.5 collective-permute-start.4
  335.2 4.5 collective-permute-start.5
  341.9 27.7 %gather_fusion.3 = f32[8192,24]{1,0:T(8,128)} fusion(f32[24,3072]{0,1:T(8,128)S(1)} %copy.200, s32[8192]{0:T(1024)S(1)} %fusion.70), kind=kCustom, calls=%fused_computation.3 | custom fusion | bytes 1605632 | tf_op jit(solution)/shard_map/gather | solution.py:66
  369.7 3.6 copy.201
  373.3 8.5 fusion.8
  381.9 6.6 add_bitcast_fusion.1
  392.1 45.1 %scatter_custom_fusion.3 = f32[24,3072]{0,1:T(8,128)S(1)} fusion(s32[8192]{0:T(1024)} %bitcast.177, f32[8192,24]{1,0:T(8,128)} %copy.205, f32[]{:T(128)} %constant.7.clone.1), kind=kCustom, calls=%fused_computation.46 | custom fusion | flops 196608 | bytes 295424 | tf_op jit(solution)/shard_map/scatter-add | solution.py:87
  437.6 6.4 collective-permute-start.6
  448.1 3.9 scatter_custom_fusion.4
  454.4 4.2 scatter_custom_fusion.5
  459.5 73.1 %psum.52 = f32[]{:T(128)} all-reduce(f32[]{:T(128)} %multiply_reduce_fusion.3), channel_id=1, replica_groups=mesh['mesh'=32,'harm'=8] {'mesh','harm'}, use_global_device_ids=true, to_apply=%region_13.14 | all-reduce | flops 1 | bytes 8 | tf_op jit(solution)/shard_map/psum | solution.py:94
  534.5 73.3 %psum.53 = f32[]{:T(128)} all-reduce(f32[]{:T(128)} %multiply_reduce_fusion.2), channel_id=1, replica_groups=mesh['mesh'=32,'harm'=8] {'mesh','harm'}, use_global_device_ids=true, to_apply=%region_15.16 | all-reduce | flops 1 | bytes 8 | tf_op jit(solution)/shard_map/psum | solution.py:78
  612.6 4.0 collective-permute-start.8
  616.6 4.0 collective-permute-start.9
  623.1 27.9 %gather_fusion.5 = f32[8192,24]{1,0:T(8,128)} fusion(f32[24,3072]{0,1:T(8,128)S(1)} %copy.212, s32[8192]{0:T(1024)S(1)} %copy-done.9), kind=kCustom, calls=%fused_computation.5 | custom fusion | bytes 1605632 | tf_op jit(solution)/shard_map/gather | solution.py:66
  651.0 3.6 copy.213
  654.6 8.5 fusion.4
  663.2 7.9 add_bitcast_fusion
  676.0 44.9 %scatter_custom_fusion.6 = f32[24,3072]{0,1:T(8,128)S(1)} fusion(s32[8192]{0:T(1024)} %bitcast.178, f32[8192,24]{1,0:T(8,128)} %copy.217, f32[]{:T(128)} %constant.7.clone.1), kind=kCustom, calls=%fused_computation.44 | custom fusion | flops 196608 | bytes 295424 | tf_op jit(solution)/shard_map/scatter-add | solution.py:87
  722.0 6.1 collective-permute-start.10
  732.6 3.9 scatter_custom_fusion.7
  738.5 4.2 scatter_custom_fusion.8
  743.7 73.3 %psum.54 = f32[]{:T(128)} all-reduce(f32[]{:T(128)} %multiply_reduce_fusion.1), channel_id=1, replica_groups=mesh['mesh'=32,'harm'=8] {'mesh','harm'}, use_global_device_ids=true, to_apply=%region_20.21 | all-reduce | flops 1 | bytes 8 | tf_op jit(solution)/shard_map/psum | solution.py:94
  825.8 5.9 collective-permute-start.13
  834.2 28.0 %gather_fusion.8 = f32[8192,4]{1,0:T(8,128)} fusion(f32[4,3072]{0,1:T(8,128)S(1)} %copy.225, s32[8192]{0:T(1024)S(1)} %copy-done.9), kind=kCustom, calls=%fused_computation.8 | custom fusion | bytes 294912 | tf_op jit(solution)/shard_map/gather | solution.py:66
  862.1 3.8 copy.226
  865.9 8.5 fusion.33
  874.4 6.6 fusion.22
  881.9 27.7 %gather_fusion.7 = f32[8192,24]{1,0:T(8,128)} fusion(f32[24,3072]{0,1:T(8,128)S(1)} %copy.223, s32[8192]{0:T(1024)S(1)} %copy-done.9), kind=kCustom, calls=%fused_computation.7 | custom fusion | bytes 1605632 | tf_op jit(solution)/shard_map/gather | solution.py:107
  913.2 9.1 gather_fusion.9
  922.3 10.0 negate_bitcast_fusion
  933.2 67.8 %all-reduce.3.cloned.1.call-done = f32[6,3,1024]{0,1,2:T(4,128)} async-done(((f32[6,3,1024]{0,1,2:T(4,128)}), f32[6,3,1024]{0,1,2:T(4,128)}) %all-reduce.3.cloned.1.call-update) | async-done | bytes 73744 | tf_op jit(solution)/shard_map/psum | solution.py:118
  (178 shorter events, 80.6 us)
Async XLA Ops:
  7.2 2.9 copy-start.25
  7.2 993.8 %all-reduce.3.cloned.1.call-start = ((), (), s32[]{:S(2)}) async-start(), calls=%async_computation | async-start | bytes 4194304 | tf_op jit(solution)/shard_map/psum | solution.py:118
  9.7 19.6 %copy-start.10 = (f32[2,6,2,2048]{3,2,1,0:T(2,128)S(1)}, f32[2,6,2,2048]{3,2,1,0:T(2,128)}, u32[]{:S(2)}) copy-start(f32[2,6,2,2048]{3,2,1,0:T(2,128)} %param.10) | copy-start | bytes 589828
  9.7 22.0 %copy-start.7 = (f32[64,64,128]{2,1,0:T(8,128)S(1)}, f32[64,64,128]{2,1,0:T(8,128)}, u32[]{:S(2)}) copy-start(f32[64,64,128]{2,1,0:T(8,128)} %param.12) | copy-start | bytes 6291460
  19.6 22.4 %collective-permute-start = (f32[24,512]{1,0:T(8,128)}, f32[24,512]{1,0:T(8,128)}, u32[]{:S(2)}, u32[]{:S(2)}) collective-permute-start(f32[24,512]{1,0:T(8,128)} %get-tuple-element.34), channel_id=1, source_target_pairs={{0,8},{8,16},{16,24},{24,32},{32,40},{40,48},{48,56},{56,64},{64,7... | collective-permute-start | bytes 147464 | tf_op jit(solution)/shard_map/ppermute | solution.py:18
  23.4 19.5 %collective-permute-start.1 = (f32[24,512]{1,0:T(8,128)}, f32[24,512]{1,0:T(8,128)}, u32[]{:S(2)}, u32[]{:S(2)}) collective-permute-start(f32[24,512]{1,0:T(8,128)} %get-tuple-element.35), channel_id=1, source_target_pairs={{8,0},{16,8},{24,16},{32,24},{40,32},{48,40},{56,48},{64,56},{72,6... | collective-permute-start | bytes 147464 | tf_op jit(solution)/shard_map/ppermute | solution.py:20
  30.8 311.1 %copy-start.8 = (s32[8192]{0:T(1024)}, s32[8192]{0:T(1024)S(1)}, u32[]{:S(2)}) copy-start(s32[8192]{0:T(1024)S(1)} %fusion.70) | copy-start | bytes 98308
  31.6 65.4 %copy-start.14 = (s32[8192,1]{0,1:T(1,128)}, s32[8192,1]{0,1:T(1,128)S(1)}, u32[]{:S(2)}) copy-start(s32[8192,1]{0,1:T(1,128)S(1)} %compare_select_fusion) | copy-start | bytes 98308
  31.6 123.3 %copy-start.27 = (s32[512,1]{0,1:T(1,128)}, s32[512,1]{0,1:T(1,128)S(1)}, u32[]{:S(2)}) copy-start(s32[512,1]{0,1:T(1,128)S(1)} %get-tuple-element.37) | copy-start | bytes 6148
  31.7 128.6 %copy-start.26 = (s32[512,1]{0,1:T(1,128)}, s32[512,1]{0,1:T(1,128)S(1)}, u32[]{:S(2)}) copy-start(s32[512,1]{0,1:T(1,128)S(1)} %get-tuple-element.36) | copy-start | bytes 6148
  31.7 123.3 %copy-start.22 = (pred[512]{0:T(512)(128)(4,1)}, pred[512]{0:T(512)(128)(4,1)S(1)}, u32[]{:S(2)}) copy-start(pred[512]{0:T(512)(128)(4,1)S(1)} %get-tuple-element.15) | copy-start | bytes 1540
  31.7 128.5 %copy-start.19 = (pred[512]{0:T(512)(128)(4,1)}, pred[512]{0:T(512)(128)(4,1)S(1)}, u32[]{:S(2)}) copy-start(pred[512]{0:T(512)(128)(4,1)S(1)} %get-tuple-element.14) | copy-start | bytes 1540
  31.7 4.5 copy-start.28
  36.4 114.6 %copy-start.15 = (f32[24]{0:T(128)}, f32[24]{0:T(128)S(1)}, u32[]{:S(2)}) copy-start(f32[24]{0:T(128)S(1)} %mul.153) | copy-start | bytes 292
  75.3 8.8 copy-start
  142.8 8.1 copy-start.12
  145.1 9.9 collective-permute-start.2
  149.0 11.2 %collective-permute-start.3 = (f32[24,512]{0,1:T(8,128)S(1)}, f32[24,512]{0,1:T(8,128)S(1)}, u32[]{:S(2)}, u32[]{:S(2)}) collective-permute-start(f32[24,512]{0,1:T(8,128)S(1)} %get-tuple-element.24), channel_id=1, source_target_pairs={{0,8},{8,16},{16,24},{24,32},{32,40},{40,48},{48,56},{56,64},{64,7... | collective-permute-start | bytes 147464 | tf_op jit(solution)/shard_map/ppermute | solution.py:30
  253.3 75.0 %copy-start.5 = (f32[24,2048]{1,0:T(8,128)}, f32[24,2048]{1,0:T(8,128)S(1)}, u32[]{:S(2)}) copy-start(f32[24,2048]{1,0:T(8,128)S(1)} %get-tuple-element.19) | copy-start | bytes 589828
  331.7 8.1 collective-permute-start.4
  335.2 6.2 collective-permute-start.5
  373.3 8.5 copy-start.1
  373.3 8.5 copy-start.16
  437.3 10.8 %copy-start.23 = (pred[512]{0:T(512)(128)(4,1)S(1)}, pred[512]{0:T(512)(128)(4,1)}, u32[]{:S(2)}) copy-start(pred[512]{0:T(512)(128)(4,1)} %copy-done.22) | copy-start | bytes 1540
  437.6 10.5 %collective-permute-start.6 = (f32[24,512]{0,1:T(8,128)S(1)}, f32[24,512]{0,1:T(8,128)S(1)}, u32[]{:S(2)}, u32[]{:S(2)}) collective-permute-start(f32[24,512]{0,1:T(8,128)S(1)} %get-tuple-element.23), channel_id=1, source_target_pairs={{8,0},{16,8},{24,16},{32,24},{40,32},{48,40},{56,48},{64,56},{72,6... | collective-permute-start | bytes 147464 | tf_op jit(solution)/shard_map/ppermute | solution.py:30
  444.0 10.4 %copy-start.20 = (pred[512]{0:T(512)(128)(4,1)S(1)}, pred[512]{0:T(512)(128)(4,1)}, u32[]{:S(2)}) copy-start(pred[512]{0:T(512)(128)(4,1)} %copy-done.19) | copy-start | bytes 1540
  444.0 10.4 %collective-permute-start.7 = (f32[24,512]{0,1:T(8,128)S(1)}, f32[24,512]{0,1:T(8,128)S(1)}, u32[]{:S(2)}, u32[]{:S(2)}) collective-permute-start(f32[24,512]{0,1:T(8,128)S(1)} %get-tuple-element.22), channel_id=1, source_target_pairs={{0,8},{8,16},{16,24},{24,32},{32,40},{40,48},{48,56},{56,64},{64,7... | collective-permute-start | bytes 147464 | tf_op jit(solution)/shard_map/ppermute | solution.py:30
  452.1 81.8 %copy-start.6 = (f32[24,2048]{1,0:T(8,128)S(1)}, f32[24,2048]{1,0:T(8,128)}, u32[]{:S(2)}) copy-start(f32[24,2048]{1,0:T(8,128)} %copy-done.5) | copy-start | bytes 589828
  612.5 10.5 %copy-start.9 = (s32[8192]{0:T(1024)S(1)}, s32[8192]{0:T(1024)}, u32[]{:S(2)}) copy-start(s32[8192]{0:T(1024)} %copy-done.8) | copy-start | bytes 98308
  612.6 8.1 collective-permute-start.8
  616.6 6.0 collective-permute-start.9
  654.6 8.5 copy-start.2
  654.6 8.5 copy-start.17
  721.7 10.9 %copy-start.24 = (pred[512]{0:T(512)(128)(4,1)S(1)}, pred[512]{0:T(512)(128)(4,1)}, u32[]{:S(2)}) copy-start(pred[512]{0:T(512)(128)(4,1)} %copy-done.22) | copy-start | bytes 1540
  722.0 10.5 %collective-permute-start.10 = (f32[24,512]{0,1:T(8,128)}, f32[24,512]{0,1:T(8,128)S(1)}, u32[]{:S(2)}, u32[]{:S(2)}) collective-permute-start(f32[24,512]{0,1:T(8,128)} %get-tuple-element.21), channel_id=1, source_target_pairs={{8,0},{16,8},{24,16},{32,24},{40,32},{48,40},{56,48},{64,56},{72,6... | collective-permute-start | bytes 147464 | tf_op jit(solution)/shard_map/ppermute | solution.py:30
  728.2 10.4 %copy-start.21 = (pred[512]{0:T(512)(128)(4,1)S(1)}, pred[512]{0:T(512)(128)(4,1)}, u32[]{:S(2)}) copy-start(pred[512]{0:T(512)(128)(4,1)} %copy-done.19) | copy-start | bytes 1540
  728.2 10.4 %collective-permute-start.11 = (f32[24,512]{0,1:T(8,128)S(1)}, f32[24,512]{0,1:T(8,128)S(1)}, u32[]{:S(2)}, u32[]{:S(2)}) collective-permute-start(f32[24,512]{0,1:T(8,128)S(1)} %get-tuple-element.20), channel_id=1, source_target_pairs={{0,8},{8,16},{16,24},{24,32},{32,40},{40,48},{48,56},{56,64},{64,7... | collective-permute-start | bytes 147464 | tf_op jit(solution)/shard_map/ppermute | solution.py:30
  736.5 7.1 copy-start.13
  818.4 5.5 copy-start.29
  818.4 5.6 copy-start.11
  821.8 9.9 collective-permute-start.12
  825.8 7.8 collective-permute-start.13
  865.9 8.5 copy-start.3
  912.6 0.7 copy-start.18
  913.2 9.1 copy-start.4
Sparse Core Ops, SparseCore 0:
  932.5 68.3 all-reduce.2
where the time goes:
time: 1020 us; the launch traced here: 1010 us
  blocking collectives  368 us (36%)
  local copies, waits for them, and re-layouts  225 us (22%)
  other arithmetic  180 us (18%)
  waiting for transfers between devices  85.9 us (8%)
  matrix products  73.3 us (7%)
  starting transfers between devices  55.7 us (5%)
  between operations  21.8 us (2%)
    psum x3, blocking collectives, squares(): return lax.psum(jnp.sum(values_now * values_now), ('mesh', 'harm'))  222 us
    psum x2, blocking collectives, per_device(): lax.psum(jnp.sum(direction * applied), ('mesh', 'harm'))  146 us
    scatter-add x3, other arithmetic, per_device(): totals.at[:, connectivity.reshape(-1)]  135 us
    gather x8, local copies, waits for them, and re-layouts, assemble(): gathered = extended[:, connectivity]  126 us
    psum x1, waiting for transfers between devices, per_device(): summed = lax.psum(local_grad, 'harm')  67.8 us
    dot_general x8, matrix products, block_product(): return jnp.einsum('ijb,rjb->rib', matrices, gathered, precision=exact_mode)  63.2 us
    gather x2, local copies, waits for them, and re-layouts, per_device(): jnp.concatenate([solution, solution_rim], axis=1)[:, connectivity]  30.6 us
    scatter-add x3, other arithmetic, per_device(): owned.at[:, safe_rows[0]]  23.8 us
  transfers between devices with their start and end apart: 15, of which 12 were waited for; matrix products, arithmetic and copies ran while one was open for 3% of the time, Pallas kernels for 0%

commit v1 on v0

--- a/solution.py
+++ b/solution.py
@@ -5,6 +5,12 @@
 
 ITERS = 3
 exact_mode = lax.Precision.HIGHEST
+
+
+def gather_and_add(block, axis):
+    parts = lax.all_gather(block, axis, axis=0, tiled=False)
+    acc = parts.sum(axis=0)
+    return acc
 
 
 def extended_2(cells, sides, width):
@@ -115,7 +121,7 @@
     )
     at_nodes = energy_term[:, :, node_block]
     local_grad = -jnp.einsum("kjn,ojn->okn", node_shape, at_nodes, precision=exact_mode)
-    summed = lax.psum(local_grad, "harm")
+    summed = gather_and_add(local_grad, "harm")
     share_size = local_grad.shape[2] // lax.axis_size("harm")
     gradient = lax.dynamic_slice_in_dim(summed, lax.axis_index("harm") * share_size, share_size, 2)
     return (solution.reshape(adjoint_rhs.shape), gradient)

time: 1020 us -> 942 us (0.924)
  waiting for transfers between devices: 85.9 us -> 18.1 us
  blocking collectives: 368 us -> 382 us
  between operations: 21.8 us -> 8.43 us
  other arithmetic: 180 us -> 169 us
    psum x1 -> x0, waiting for transfers between devices: 67.8 us -> none  [per_device(): summed = lax.psum(local_grad, 'harm')]
    all_gather x0 -> x1, blocking collectives: none -> 13.5 us  [gather_and_add(): parts = lax.all_gather(block, axis, axis=0, tiled=False)]
    scatter-add x3, other arithmetic: 23.8 us -> 12.7 us  [per_device(): owned.at[:, safe_rows[0]]]
  transfers between devices with their start and end apart: 15 -> 14, of which waited for: 12 -> 11; matrix products, arithmetic and copies ran while one was open for 3% -> 3% of each run, Pallas kernels for 0% -> 0%
where the time goes in v1:
time: 942 us; the launch traced here: 932 us
  blocking collectives  382 us (41%)
  local copies, waits for them, and re-layouts  226 us (24%)
  other arithmetic  169 us (18%)
  matrix products  73.5 us (8%)
  starting transfers between devices  55.6 us (6%)
  waiting for transfers between devices  18.1 us (2%)
    psum x3, blocking collectives, squares(): return lax.psum(jnp.sum(values_now * values_now), ('mesh', 'harm'))  222 us
    psum x2, blocking collectives, per_device(): lax.psum(jnp.sum(direction * applied), ('mesh', 'harm'))  146 us
    scatter-add x3, other arithmetic, per_device(): totals.at[:, connectivity.reshape(-1)]  135 us
    gather x8, local copies, waits for them, and re-layouts, assemble(): gathered = extended[:, connectivity]  126 us
    dot_general x8, matrix products, block_product(): return jnp.einsum('ijb,rjb->rib', matrices, gathered, precision=exact_mode)  63.5 us
    gather x2, local copies, waits for them, and re-layouts, per_device(): jnp.concatenate([solution, solution_rim], axis=1)[:, connectivity]  30.6 us
    ppermute x6, starting transfers between devices, from_behind(): return lax.ppermute(shard, axis, pairs)  22.1 us
    ppermute x4, starting transfers between devices, extended_2(): lax.ppermute(head, axis, [((i + 1) % count, i) for i in range(ends)])  20.2 us
  transfers between devices with their start and end apart: 14, of which 11 were waited for; matrix products, arithmetic and copies ran while one was open for 3% of the time, Pallas kernels for 0%

profile of v1, /device:TPU:2, one launch (start us, length us, event | category | flops | bytes accessed | tf_op | source)
XLA Modules:
  0.0 932.3 jit_solution(9627047979161966027)
XLA Ops:
  4.1 4.0 gather_fusion
  13.0 3.8 collective-permute-start
  16.8 5.8 collective-permute-start.1
  25.2 4.5 copy.195
  29.8 5.6 copy.196
  37.4 27.7 %gather_fusion.1 = f32[8192,24]{1,0:T(8,128)} fusion(f32[24,3072]{0,1:T(8,128)S(1)} %pad_maximum_fusion, s32[8192]{0:T(1024)S(1)} %fusion.70), kind=kCustom, calls=%fused_computation.1 | custom fusion | bytes 1605632 | tf_op jit(solution)/shard_map/gather | solution.py:72
  65.1 3.6 copy.194
  68.8 9.0 fusion.12
  77.8 7.9 add_bitcast_fusion.2
  90.7 44.7 %scatter_custom_fusion = f32[24,3072]{0,1:T(8,128)S(1)} fusion(s32[8192]{0:T(1024)S(1)} %bitcast.178, f32[8192,24]{1,0:T(8,128)} %copy.198, f32[]{:T(128)} %constant.7.clone.1), kind=kCustom, calls=%fused_computation.48 | custom fusion | flops 196608 | bytes 295424 | tf_op jit(solution)/shard_map/scatter-add | solution.py:93
  138.8 3.9 collective-permute-start.2
  145.1 3.6 collective-permute-done.2
  148.7 3.8 scatter_custom_fusion.1
  153.9 4.3 scatter_custom_fusion.2
  159.4 74.6 %all-reduce = (f32[]{:T(128)}, f32[]{:T(128)}) all-reduce(f32[]{:T(128)} %multiply_reduce_fusion.5, f32[]{:T(128)} %multiply_reduce_fusion), channel_id=1, replica_groups=mesh['mesh'=32,'harm'=8] {'mesh','harm'}, use_global_device_ids=true, to_apply=%region_1.2 | all-reduce | flops 2 | bytes 16 | tf_op jit(solution)/shard_map/psum | solution.py:84
  235.8 73.8 %psum.44 = f32[]{:T(128)} all-reduce(f32[]{:T(128)} %get-tuple-element.16), channel_id=1, replica_groups=mesh['mesh'=32,'harm'=8] {'mesh','harm'}, use_global_device_ids=true, to_apply=%region_8.9 | all-reduce | flops 1 | bytes 8 | tf_op jit(solution)/shard_map/psum | solution.py:84
  314.2 3.5 collective-permute-start.4
  317.7 4.5 collective-permute-start.5
  324.4 27.7 %gather_fusion.3 = f32[8192,24]{1,0:T(8,128)} fusion(f32[24,3072]{0,1:T(8,128)S(1)} %copy.205, s32[8192]{0:T(1024)S(1)} %fusion.70), kind=kCustom, calls=%fused_computation.3 | custom fusion | bytes 1605632 | tf_op jit(solution)/shard_map/gather | solution.py:72
  352.2 3.6 copy.206
  355.8 8.5 fusion.8
  364.4 6.6 add_bitcast_fusion.1
  374.6 45.1 %scatter_custom_fusion.3 = f32[24,3072]{0,1:T(8,128)S(1)} fusion(s32[8192]{0:T(1024)} %bitcast.179, f32[8192,24]{1,0:T(8,128)} %copy.210, f32[]{:T(128)} %constant.7.clone.1), kind=kCustom, calls=%fused_computation.46 | custom fusion | flops 196608 | bytes 295424 | tf_op jit(solution)/shard_map/scatter-add | solution.py:93
  420.1 6.4 collective-permute-start.6
  430.6 3.9 scatter_custom_fusion.4
  436.9 4.2 scatter_custom_fusion.5
  442.0 73.1 %psum.45 = f32[]{:T(128)} all-reduce(f32[]{:T(128)} %multiply_reduce_fusion.3), channel_id=1, replica_groups=mesh['mesh'=32,'harm'=8] {'mesh','harm'}, use_global_device_ids=true, to_apply=%region_13.14 | all-reduce | flops 1 | bytes 8 | tf_op jit(solution)/shard_map/psum | solution.py:100
  517.0 73.3 %psum.46 = f32[]{:T(128)} all-reduce(f32[]{:T(128)} %multiply_reduce_fusion.2), channel_id=1, replica_groups=mesh['mesh'=32,'harm'=8] {'mesh','harm'}, use_global_device_ids=true, to_apply=%region_15.16 | all-reduce | flops 1 | bytes 8 | tf_op jit(solution)/shard_map/psum | solution.py:84
  595.1 4.0 collective-permute-start.8
  599.1 4.0 collective-permute-start.9
  605.6 27.9 %gather_fusion.5 = f32[8192,24]{1,0:T(8,128)} fusion(f32[24,3072]{0,1:T(8,128)S(1)} %copy.217, s32[8192]{0:T(1024)S(1)} %copy-done.9), kind=kCustom, calls=%fused_computation.5 | custom fusion | bytes 1605632 | tf_op jit(solution)/shard_map/gather | solution.py:72
  633.5 3.6 copy.218
  637.1 8.5 fusion.4
  645.7 7.9 add_bitcast_fusion
  658.5 44.9 %scatter_custom_fusion.6 = f32[24,3072]{0,1:T(8,128)S(1)} fusion(s32[8192]{0:T(1024)} %bitcast.180, f32[8192,24]{1,0:T(8,128)} %copy.222, f32[]{:T(128)} %constant.7.clone.1), kind=kCustom, calls=%fused_computation.44 | custom fusion | flops 196608 | bytes 295424 | tf_op jit(solution)/shard_map/scatter-add | solution.py:93
  704.6 6.1 collective-permute-start.10
  715.1 3.9 scatter_custom_fusion.7
  721.0 4.2 scatter_custom_fusion.8
  726.2 73.3 %psum.47 = f32[]{:T(128)} all-reduce(f32[]{:T(128)} %multiply_reduce_fusion.1), channel_id=1, replica_groups=mesh['mesh'=32,'harm'=8] {'mesh','harm'}, use_global_device_ids=true, to_apply=%region_20.21 | all-reduce | flops 1 | bytes 8 | tf_op jit(solution)/shard_map/psum | solution.py:100
  809.1 5.9 collective-permute-start.13
  817.5 28.0 %gather_fusion.8 = f32[8192,4]{1,0:T(8,128)} fusion(f32[4,3072]{0,1:T(8,128)S(1)} %copy.230, s32[8192]{0:T(1024)S(1)} %copy-done.9), kind=kCustom, calls=%fused_computation.8 | custom fusion | bytes 294912 | tf_op jit(solution)/shard_map/gather | solution.py:72
  845.4 3.8 copy.231
  849.2 8.5 fusion.33
  857.7 6.6 fusion.22
  865.2 27.7 %gather_fusion.7 = f32[8192,24]{1,0:T(8,128)} fusion(f32[24,3072]{0,1:T(8,128)S(1)} %copy.228, s32[8192]{0:T(1024)S(1)} %copy-done.9), kind=kCustom, calls=%fused_computation.7 | custom fusion | bytes 1605632 | tf_op jit(solution)/shard_map/gather | solution.py:113
  896.5 9.1 gather_fusion.9
  905.6 10.0 %negate_bitcast_fusion = f32[6,3,1024]{0,1,2:T(4,128)} fusion(f32[3,64,1024]{1,0,2:T(4,128)S(1)} %copy-done.4, f32[1024,6,64]{2,1,0:T(8,128)} %gather_fusion.9), kind=kOutput, calls=%fused_computation.21 | convolution fusion | flops 14174208 | bytes 2433024 | tf_op jit(solution)/shard_map/kjn,ojn->okn/dot_general | solution.py:123
  917.6 13.5 %all-gather = f32[48,3,1024]{2,1,0:T(4,128)S(1)} all-gather(f32[6,3,1024]{2,1,0:T(4,128)S(1)} %copy.238), channel_id=2, replica_groups=mesh['mesh'=32,'harm'=8] {'harm'}, dimensions={0}, use_global_device_ids=true | all-gather | bytes 663552 | tf_op jit(solution)/shard_map/all_gather | solution.py:11
  (177 shorter events, 81.5 us)
Async XLA Ops:
  0.6 2.8 copy-start.25
  3.1 19.6 %copy-start.10 = (f32[2,6,2,2048]{3,2,1,0:T(2,128)S(1)}, f32[2,6,2,2048]{3,2,1,0:T(2,128)}, u32[]{:S(2)}) copy-start(f32[2,6,2,2048]{3,2,1,0:T(2,128)} %param.10) | copy-start | bytes 589828
  3.1 22.0 %copy-start.7 = (f32[64,64,128]{2,1,0:T(8,128)S(1)}, f32[64,64,128]{2,1,0:T(8,128)}, u32[]{:S(2)}) copy-start(f32[64,64,128]{2,1,0:T(8,128)} %param.12) | copy-start | bytes 6291460
  13.0 22.4 %collective-permute-start = (f32[24,512]{1,0:T(8,128)}, f32[24,512]{1,0:T(8,128)}, u32[]{:S(2)}, u32[]{:S(2)}) collective-permute-start(f32[24,512]{1,0:T(8,128)} %get-tuple-element.32), channel_id=1, source_target_pairs={{0,8},{8,16},{16,24},{24,32},{32,40},{40,48},{48,56},{56,64},{64,7... | collective-permute-start | bytes 147464 | tf_op jit(solution)/shard_map/ppermute | solution.py:24
  16.8 19.5 %collective-permute-start.1 = (f32[24,512]{1,0:T(8,128)}, f32[24,512]{1,0:T(8,128)}, u32[]{:S(2)}, u32[]{:S(2)}) collective-permute-start(f32[24,512]{1,0:T(8,128)} %get-tuple-element.33), channel_id=1, source_target_pairs={{8,0},{16,8},{24,16},{32,24},{40,32},{48,40},{56,48},{64,56},{72,6... | collective-permute-start | bytes 147464 | tf_op jit(solution)/shard_map/ppermute | solution.py:26
  24.2 300.2 %copy-start.8 = (s32[8192]{0:T(1024)}, s32[8192]{0:T(1024)S(1)}, u32[]{:S(2)}) copy-start(s32[8192]{0:T(1024)S(1)} %fusion.70) | copy-start | bytes 98308
  25.0 65.6 %copy-start.14 = (s32[8192,1]{0,1:T(1,128)}, s32[8192,1]{0,1:T(1,128)S(1)}, u32[]{:S(2)}) copy-start(s32[8192,1]{0,1:T(1,128)S(1)} %compare_select_fusion) | copy-start | bytes 98308
  25.1 123.6 %copy-start.27 = (s32[512,1]{0,1:T(1,128)}, s32[512,1]{0,1:T(1,128)S(1)}, u32[]{:S(2)}) copy-start(s32[512,1]{0,1:T(1,128)S(1)} %get-tuple-element.35) | copy-start | bytes 6148
  25.1 128.9 %copy-start.26 = (s32[512,1]{0,1:T(1,128)}, s32[512,1]{0,1:T(1,128)S(1)}, u32[]{:S(2)}) copy-start(s32[512,1]{0,1:T(1,128)S(1)} %get-tuple-element.34) | copy-start | bytes 6148
  25.1 123.5 %copy-start.22 = (pred[512]{0:T(512)(128)(4,1)}, pred[512]{0:T(512)(128)(4,1)S(1)}, u32[]{:S(2)}) copy-start(pred[512]{0:T(512)(128)(4,1)S(1)} %get-tuple-element.13) | copy-start | bytes 1540
  25.1 128.8 %copy-start.19 = (pred[512]{0:T(512)(128)(4,1)}, pred[512]{0:T(512)(128)(4,1)S(1)}, u32[]{:S(2)}) copy-start(pred[512]{0:T(512)(128)(4,1)S(1)} %get-tuple-element.12) | copy-start | bytes 1540
  25.2 4.5 copy-start.28
  29.8 114.8 %copy-start.15 = (f32[24]{0:T(128)}, f32[24]{0:T(128)S(1)}, u32[]{:S(2)}) copy-start(f32[24]{0:T(128)S(1)} %mul.153) | copy-start | bytes 292
  68.8 9.1 copy-start
  136.5 8.1 copy-start.12
  138.8 9.9 %collective-permute-start.2 = (f32[24,512]{0,1:T(8,128)}, f32[24,512]{0,1:T(8,128)S(1)}, u32[]{:S(2)}, u32[]{:S(2)}) collective-permute-start(f32[24,512]{0,1:T(8,128)} %get-tuple-element.23), channel_id=1, source_target_pairs={{8,0},{16,8},{24,16},{32,24},{40,32},{48,40},{56,48},{64,56},{72,6... | collective-permute-start | bytes 147464 | tf_op jit(solution)/shard_map/ppermute | solution.py:36
  142.7 11.2 %collective-permute-start.3 = (f32[24,512]{0,1:T(8,128)S(1)}, f32[24,512]{0,1:T(8,128)S(1)}, u32[]{:S(2)}, u32[]{:S(2)}) collective-permute-start(f32[24,512]{0,1:T(8,128)S(1)} %get-tuple-element.22), channel_id=1, source_target_pairs={{0,8},{8,16},{16,24},{24,32},{32,40},{40,48},{48,56},{56,64},{64,7... | collective-permute-start | bytes 147464 | tf_op jit(solution)/shard_map/ppermute | solution.py:36
  235.8 75.0 %copy-start.5 = (f32[24,2048]{1,0:T(8,128)}, f32[24,2048]{1,0:T(8,128)S(1)}, u32[]{:S(2)}) copy-start(f32[24,2048]{1,0:T(8,128)S(1)} %get-tuple-element.17) | copy-start | bytes 589828
  314.2 8.1 collective-permute-start.4
  317.7 6.2 collective-permute-start.5
  355.8 8.5 copy-start.1
  355.8 8.5 copy-start.16
  419.8 10.8 %copy-start.23 = (pred[512]{0:T(512)(128)(4,1)S(1)}, pred[512]{0:T(512)(128)(4,1)}, u32[]{:S(2)}) copy-start(pred[512]{0:T(512)(128)(4,1)} %copy-done.22) | copy-start | bytes 1540
  420.1 10.5 %collective-permute-start.6 = (f32[24,512]{0,1:T(8,128)S(1)}, f32[24,512]{0,1:T(8,128)S(1)}, u32[]{:S(2)}, u32[]{:S(2)}) collective-permute-start(f32[24,512]{0,1:T(8,128)S(1)} %get-tuple-element.21), channel_id=1, source_target_pairs={{8,0},{16,8},{24,16},{32,24},{40,32},{48,40},{56,48},{64,56},{72,6... | collective-permute-start | bytes 147464 | tf_op jit(solution)/shard_map/ppermute | solution.py:36
  426.5 10.4 %copy-start.20 = (pred[512]{0:T(512)(128)(4,1)S(1)}, pred[512]{0:T(512)(128)(4,1)}, u32[]{:S(2)}) copy-start(pred[512]{0:T(512)(128)(4,1)} %copy-done.19) | copy-start | bytes 1540
  426.5 10.4 %collective-permute-start.7 = (f32[24,512]{0,1:T(8,128)S(1)}, f32[24,512]{0,1:T(8,128)S(1)}, u32[]{:S(2)}, u32[]{:S(2)}) collective-permute-start(f32[24,512]{0,1:T(8,128)S(1)} %get-tuple-element.20), channel_id=1, source_target_pairs={{0,8},{8,16},{16,24},{24,32},{32,40},{40,48},{48,56},{56,64},{64,7... | collective-permute-start | bytes 147464 | tf_op jit(solution)/shard_map/ppermute | solution.py:36
  434.6 81.8 %copy-start.6 = (f32[24,2048]{1,0:T(8,128)S(1)}, f32[24,2048]{1,0:T(8,128)}, u32[]{:S(2)}) copy-start(f32[24,2048]{1,0:T(8,128)} %copy-done.5) | copy-start | bytes 589828
  595.0 10.5 %copy-start.9 = (s32[8192]{0:T(1024)S(1)}, s32[8192]{0:T(1024)}, u32[]{:S(2)}) copy-start(s32[8192]{0:T(1024)} %copy-done.8) | copy-start | bytes 98308
  595.1 8.1 collective-permute-start.8
  599.1 6.0 collective-permute-start.9
  637.1 8.5 copy-start.2
  637.1 8.5 copy-start.17
  704.3 10.9 %copy-start.24 = (pred[512]{0:T(512)(128)(4,1)S(1)}, pred[512]{0:T(512)(128)(4,1)}, u32[]{:S(2)}) copy-start(pred[512]{0:T(512)(128)(4,1)} %copy-done.22) | copy-start | bytes 1540
  704.6 10.5 %collective-permute-start.10 = (f32[24,512]{0,1:T(8,128)}, f32[24,512]{0,1:T(8,128)S(1)}, u32[]{:S(2)}, u32[]{:S(2)}) collective-permute-start(f32[24,512]{0,1:T(8,128)} %get-tuple-element.19), channel_id=1, source_target_pairs={{8,0},{16,8},{24,16},{32,24},{40,32},{48,40},{56,48},{64,56},{72,6... | collective-permute-start | bytes 147464 | tf_op jit(solution)/shard_map/ppermute | solution.py:36
  710.7 10.4 %copy-start.21 = (pred[512]{0:T(512)(128)(4,1)S(1)}, pred[512]{0:T(512)(128)(4,1)}, u32[]{:S(2)}) copy-start(pred[512]{0:T(512)(128)(4,1)} %copy-done.19) | copy-start | bytes 1540
  710.7 10.4 %collective-permute-start.11 = (f32[24,512]{0,1:T(8,128)S(1)}, f32[24,512]{0,1:T(8,128)S(1)}, u32[]{:S(2)}, u32[]{:S(2)}) collective-permute-start(f32[24,512]{0,1:T(8,128)S(1)} %get-tuple-element.18), channel_id=1, source_target_pairs={{0,8},{8,16},{16,24},{24,32},{32,40},{40,48},{48,56},{56,64},{64,7... | collective-permute-start | bytes 147464 | tf_op jit(solution)/shard_map/ppermute | solution.py:36
  719.0 7.1 copy-start.13
  800.9 5.5 copy-start.29
  800.9 5.6 copy-start.11
  804.3 10.7 %collective-permute-start.12 = (f32[28,512]{1,0:T(8,128)S(1)}, f32[28,512]{1,0:T(8,128)S(1)}, u32[]{:S(2)}, u32[]{:S(2)}) collective-permute-start(f32[28,512]{1,0:T(8,128)S(1)} %get-tuple-element.27), channel_id=1, source_target_pairs={{0,8},{8,16},{16,24},{24,32},{32,40},{40,48},{48,56},{56,64},{64,7... | collective-permute-start | bytes 172040 | tf_op jit(solution)/shard_map/ppermute | solution.py:24
  809.1 7.8 collective-permute-start.13
  849.2 8.5 copy-start.3
  895.8 0.7 copy-start.18
  896.5 9.1 copy-start.4
